TPU v7x, 128 devices: a whole 4x4x4 slice. The times are simulated.
128 devices in a mesh: space: 8 (over z, y_lo), vel: 16 (over y_hi, x, core).
Axes of the slice: x: 4, y: 4 (y_hi: 2, y_lo: 2; y = y_hi * 2 + y_lo), z: 4, core: 2. Of those that a mesh axis runs over, the one named last changes fastest.
Arguments:
- distribution: bfloat16 [4096, 48, 8, 128], P('vel', 'space'), may hold values from -6 to 6
- up_factor: bfloat16 [4096, 256], P('vel'), may hold values from -0.75 to 0.75
- down_factor: bfloat16 [4096, 256], P('vel'), may hold values from -0.09375 to 0.09375
- decay: float32 [4096], P('vel'), may hold values from 0.3 to 3
- wall_kind: int32 [2, 8, 128], replicated, may hold values from 0 to 2
Outputs:
- advanced: bfloat16 [4096, 48, 8, 128], P('vel', 'space')
Inputs may be any that keep to these rules, and one draw needn't show every extreme that they name: `wall_kind`: 0 marks a diffuse wall at rest, 1 a diffuse heated wall, 2 an open face.
All inputs are finite; a program needn't handle non-finite values.
Results may differ from a plain program's by a relative error of at most 0.0046.
Values may be sent and summed in bfloat16 or wider, within the bound.
A program may use at most 192 MiB of HBM per device.

v0:
```python
import jax
import jax.numpy as jnp
from jax import lax
from jax.sharding import PartitionSpec as P

NV = 16
STEPS = 2
speed_range = 8.0
time_ratio = 0.08
wall_heat = 3.0


def with_halo(block, sides, width):
    for axis, dim in sides:
        count = lax.axis_size(axis)
        forward = [(i, i + 1) for i in range(count - 1)]
        backward = [(target, source) for source, target in forward]
        low = lax.ppermute(
            lax.slice_in_dim(block, block.shape[dim] - width, None, axis=dim), axis, forward
        )
        high = lax.ppermute(lax.slice_in_dim(block, 0, width, axis=dim), axis, backward)
        block = jnp.concatenate([low, block, high], axis=dim)
    return block


def components(vel_ids):
    spacing = speed_range / NV
    midpoint = (NV - 1) / 2.0
    along_z = ((vel_ids // (NV * NV)).astype(jnp.float32) - midpoint) * spacing
    along_x = ((vel_ids // NV % NV).astype(jnp.float32) - midpoint) * spacing
    along_y = ((vel_ids % NV).astype(jnp.float32) - midpoint) * spacing
    return (along_z, along_x, along_y)


def wall_ghost(outflux, kind_face, maxwell, energy, norm):
    sigma = outflux / norm
    heating = jnp.where(kind_face == 1, wall_heat, 0.0)
    opened = jnp.where(kind_face == 2, 0.0, 1.0)
    return (
        maxwell[:, None, None]
        * (sigma[None] + heating[None] * energy[:, None, None])
        * opened[None]
    )


def transport(centre, lower_plane, upper_plane, along_z, along_x, along_y):
    dimensions = centre.ndim
    shaped = (-1,) + (1,) * (dimensions - 1)
    axis_x = dimensions - 2
    axis_y = dimensions - 1
    plus_z = jnp.maximum(along_z, 0.0).reshape(shaped)
    minus_z = jnp.minimum(along_z, 0.0).reshape(shaped)
    plus_x = jnp.maximum(along_x, 0.0).reshape(shaped)
    minus_x = jnp.minimum(along_x, 0.0).reshape(shaped)
    plus_y = jnp.maximum(along_y, 0.0).reshape(shaped)
    minus_y = jnp.minimum(along_y, 0.0).reshape(shaped)
    result = plus_z * (centre - lower_plane) + minus_z * (upper_plane - centre)
    result = (
        result
        + plus_x * (centre - jnp.roll(centre, 1, axis_x))
        + minus_x * (jnp.roll(centre, -1, axis_x) - centre)
    )
    result = (
        result
        + plus_y * (centre - jnp.roll(centre, 1, axis_y))
        + minus_y * (jnp.roll(centre, -1, axis_y) - centre)
    )
    return result


def body(distribution, up_factor, down_factor, decay, wall_kind):
    local_vel, depth, width_x, width_y = distribution.shape
    cells = depth * width_x * width_y
    vel_ids = lax.axis_index("vel") * local_vel + jnp.arange(local_vel, dtype=jnp.int32)
    along_z, along_x, along_y = components(vel_ids)
    speed_sq = along_z * along_z + along_x * along_x + along_y * along_y
    maxwell = jnp.exp(-0.5 * speed_sq)
    energy = 0.5 * speed_sq - 1.5
    all_ids = jnp.arange(NV**3, dtype=jnp.int32)
    full_z, full_x, full_y = components(all_ids)
    norm = jnp.sum(
        jnp.maximum(full_z, 0.0)
        * jnp.exp(-0.5 * (full_z * full_z + full_x * full_x + full_y * full_y))
    )
    slab = lax.axis_index("space")
    slabs = lax.axis_size("space")
    current = distribution
    for step in range(STEPS):
        low_face = current[:, 0].astype(jnp.float32)
        high_face = current[:, depth - 1].astype(jnp.float32)
        out_low = jnp.sum(jnp.maximum(-along_z, 0.0)[:, None, None] * low_face, axis=0)
        out_high = jnp.sum(jnp.maximum(along_z, 0.0)[:, None, None] * high_face, axis=0)
        outflux = lax.psum(jnp.stack([out_low, out_high]), "vel")
        ghost_low = wall_ghost(outflux[0], wall_kind[0], maxwell, energy, norm)
        ghost_high = wall_ghost(outflux[1], wall_kind[1], maxwell, energy, norm)
        padded = with_halo(current, (("space", 1),), 1)
        first_plane = jnp.where(slab == 0, ghost_low, padded[:, 0].astype(jnp.float32))
        last_plane = jnp.where(
            slab == slabs - 1, ghost_high, padded[:, depth + 1].astype(jnp.float32)
        )
        lower_plane = jnp.concatenate(
            [first_plane[:, None], padded[:, 1:depth].astype(jnp.float32)], axis=1
        )
        upper_plane = jnp.concatenate(
            [padded[:, 2 : depth + 1].astype(jnp.float32), last_plane[:, None]], axis=1
        )
        centre = current.astype(jnp.float32)
        moved = transport(centre, lower_plane, upper_plane, along_z, along_x, along_y)
        flat_rows = current.reshape(local_vel, cells)
        coeffs = lax.psum_scatter(
            lax.dot_general(
                flat_rows, down_factor, (((0,), (0,)), ((), ())), preferred_element_type=jnp.float32
            ),
            "vel",
            scatter_dimension=0,
            tiled=True,
        ).astype(jnp.bfloat16)
        gained = lax.dot_general(
            up_factor,
            lax.all_gather(coeffs, "vel", axis=0, tiled=True),
            (((1,), (1,)), ((), ())),
            preferred_element_type=jnp.float32,
        ).reshape(current.shape)
        updated = (
            centre
            - time_ratio * moved
            + time_ratio * (gained - decay[:, None, None, None] * centre)
        )
        current = updated.astype(jnp.bfloat16)
    return current


def solution(mesh):
    return jax.shard_map(
        body,
        mesh=mesh,
        in_specs=(P("vel", "space", None, None), P("vel", None), P("vel", None), P("vel"), P()),
        out_specs=P("vel", "space", None, None),
        check_vma=False,
    )
```

profile of v0, /device:TPU:8, one launch (start us, length us, event | category | flops | bytes accessed | tf_op | source)
XLA Modules:
  0.0 419.7 jit_solution(15023858921832519522)
XLA Ops:
  6.5 0.0 copy-start
  6.5 0.0 reduce-scatter.3.cloned.1.call-start
  6.5 0.9 copy-done
  7.4 5.9 %fusion.35 = f32[6144,256]{1,0:T(8,128)} fusion(bf16[256,256]{1,0:T(8,128)(2,1)S(1)} %copy-done, bf16[32,8,48,128]{3,2,1,0:T(8,128)(2,1)} %bitcast.76), kind=kOutput, calls=%fused_computation.51 | convolution fusion | flops 805306368 | bytes 9568256 | tf_op jit(solution)/shard_map/dot_general | solution.py:111
  13.3 0.0 copy-start.2
  13.3 0.0 reduce-scatter.3.cloned.1.call-update
  13.3 0.0 all-gather.3.cloned.1.call-start
  13.4 91.1 %reduce-scatter.3.cloned.1.call-done = f32[384,256]{1,0:T(8,128)} async-done(((f32[6144,256]{1,0:T(8,128)}), f32[384,256]{1,0:T(8,128)}) %reduce-scatter.3.cloned.1.call-update) | async-done | bytes 393232 | tf_op jit(solution)/shard_map/reduce_scatter | solution.py:110
  104.5 1.7 convert_element_type.151
  106.2 0.0 all-gather.3.cloned.1.call-update
  106.2 0.0 reduce-scatter.5.cloned.1.call-start
  106.3 0.0 copy-done.2
  106.3 1.1 slice_bitcast_fusion.2
  107.4 4.3 %collective-permute-start = (bf16[256,1,8,128]{3,2,0,1:T(8,128)(2,1)}, bf16[256,1,8,128]{3,2,0,1:T(8,128)(2,1)}, u32[]{:S(2)}, u32[]{:S(2)}) collective-permute-start(bf16[256,1,8,128]{3,2,0,1:T(8,128)(2,1)} %get-tuple-element.21), channel_id=1, source_target_pairs={{0,16},{16,32},{32,48},{48,64},{64,80},{80,96},{96,112},{1,17},{17... | collective-permute-start | bytes 1572872 | tf_op jit(solution)/shard_map/ppermute | solution.py:18
  111.7 2.3 collective-permute-start.1
  114.0 0.7 fusion.86
  114.7 1.0 fusion.57
  115.7 34.9 %psum.14 = f32[2,8,128]{2,1,0:T(8,128)S(1)} all-reduce(f32[2,8,128]{2,1,0:T(8,128)S(1)} %pad_maximum_fusion), channel_id=1, replica_groups=mesh['space'=8,'vel'=16] {'vel'}, use_global_device_ids=true, to_apply=%region_2.3 | all-reduce | flops 2048 | bytes 16384 | tf_op jit(solution)/shard_map/psum | solution.py:93
  150.7 4.7 %slice_convert_fusion.3 = (f32[256,5,8,128]{3,2,1,0:T(8,128)}, f32[256,5,8,128]{3,2,1,0:T(8,128)}) fusion(bf16[256,6,8,128]{3,2,1,0:T(8,128)(2,1)S(1)} %copy-done.2), kind=kLoop, calls=%fused_computation.57 | loop fusion | flops 2621440 | bytes 15728640 | tf_op jit(solution)/shard_map/convert_element_type | solution.py:102
  155.4 2.1 fusion.103
  157.5 5.5 %fusion.106 = (f32[256,6,8,127]{3,2,1,0:T(8,128)}, f32[256,6,8,127]{3,2,1,0:T(8,128)}) fusion(bf16[256,6,8,128]{3,2,1,0:T(8,128)(2,1)S(1)} %copy-done.2), kind=kLoop, calls=%fused_computation.182 | loop fusion | bytes 24969216 | tf_op jit(solution)/shard_map/jit(_roll_static)/slice | solution.py:65
  163.0 5.5 %fusion.105 = (f32[256,6,8,1]{3,2,1,0:T(8,128)}, f32[256,6,8,1]{3,2,1,0:T(8,128)}) fusion(bf16[256,6,8,128]{3,2,1,0:T(8,128)(2,1)S(1)} %copy-done.2), kind=kLoop, calls=%fused_computation.181 | loop fusion | bytes 196608 | tf_op jit(solution)/shard_map/jit(_roll_static)/slice | solution.py:65
  168.4 0.0 copy-start.4
  168.4 0.0 copy-start.3
  168.5 5.4 %fusion.104 = (f32[256,6,7,128]{3,2,1,0:T(8,128)}, f32[256,6,7,128]{3,2,1,0:T(8,128)}) fusion(bf16[256,6,8,128]{3,2,1,0:T(8,128)(2,1)S(1)} %copy-done.2), kind=kLoop, calls=%fused_computation.180 | loop fusion | bytes 22020096 | tf_op jit(solution)/shard_map/jit(_roll_static)/slice | solution.py:60
  173.9 0.6 fusion.90
  174.5 0.0 copy-done.4
  174.6 0.0 collective-permute-done
  174.6 2.6 fusion.41
  177.2 0.0 collective-permute-done.1
  177.2 2.6 fusion.49
  179.8 0.0 all-gather.3.cloned.1.call-done
  179.8 0.0 copy-done.3
  179.8 5.5 %fusion.107 = f32[6144,256]{1,0:T(8,128)} fusion(bf16[6144,256]{1,0:T(8,128)(2,1)} %all-gather.3.cloned.1.call-done, bf16[256,256]{1,0:T(8,128)(2,1)S(1)} %copy-done.3), kind=kOutput, calls=%fused_computation.183 | convolution fusion | flops 805306368 | bytes 9568256 | tf_op jit(solution)/shard_map/dot_general | solution.py:118
  185.3 0.0 copy-start.5
  185.3 6.7 %copy.10 = f32[256,6,8,128]{3,2,1,0:T(8,128)} copy(f32[256,6,8,128]{0,3,2,1:T(8,128)} %bitcast.77) | data formatting | bytes 12582912 | tf_op jit(solution)/shard_map/reshape | solution.py:123
  192.0 0.0 copy-done.5
  192.0 21.8 %fusion.31 = bf16[256,6,8,128]{3,2,1,0:T(8,128)(2,1)S(1)} fusion(f32[256,6,8,128]{3,2,1,0:T(8,128)} %copy.10, f32[256,6,8,1]{3,2,1,0:T(8,128)} %get-tuple-element.30, f32[256,6,8,127]{3,2,1,0:T(8,128)} %get-tuple-element.32, f32[256,6,8,127]{3,2,1,0:T(8,128)} %get-tuple-element.31, f32[256,6,8,1]{3,2,1,0:T(8,128)} %get-tuple-element.29, ...), kind=kLoop, calls=%fused_computation.47 | loop fusion | flops 48758784 | bytes 50338816 | tf_op jit(solution)/shard_map/convert_element_type | solution.py:129
  213.8 4.0 fusion.32
  217.8 0.0 reduce-scatter.5.cloned.1.call-update
  217.8 0.0 all-gather.5.cloned.1.call-start
  217.8 87.7 %reduce-scatter.5.cloned.1.call-done = f32[384,256]{1,0:T(8,128)} async-done(((f32[6144,256]{1,0:T(8,128)}), f32[384,256]{1,0:T(8,128)}) %reduce-scatter.5.cloned.1.call-update) | async-done | bytes 393232 | tf_op jit(solution)/shard_map/reduce_scatter | solution.py:110
  305.6 1.7 convert_element_type.162
  307.3 0.0 all-gather.5.cloned.1.call-update
  307.3 1.0 slice_bitcast_fusion
  308.3 4.3 %collective-permute-start.2 = (bf16[256,1,8,128]{3,2,0,1:T(8,128)(2,1)}, bf16[256,1,8,128]{3,2,0,1:T(8,128)(2,1)}, u32[]{:S(2)}, u32[]{:S(2)}) collective-permute-start(bf16[256,1,8,128]{3,2,0,1:T(8,128)(2,1)} %get-tuple-element.9), channel_id=1, source_target_pairs={{0,16},{16,32},{32,48},{48,64},{64,80},{80,96},{96,112},{1,17},{17... | collective-permute-start | bytes 1572872 | tf_op jit(solution)/shard_map/ppermute | solution.py:18
  312.7 2.3 collective-permute-start.3
  315.0 1.0 fusion.55
  316.0 35.1 %psum.15 = f32[2,8,128]{2,1,0:T(8,128)S(1)} all-reduce(f32[2,8,128]{2,1,0:T(8,128)S(1)} %pad_maximum_fusion.1), channel_id=1, replica_groups=mesh['space'=8,'vel'=16] {'vel'}, use_global_device_ids=true, to_apply=%region_7.8 | all-reduce | flops 2048 | bytes 16384 | tf_op jit(solution)/shard_map/psum | solution.py:93
  351.0 0.6 fusion.88
  351.7 2.1 fusion.99
  353.8 5.6 %fusion.102 = (f32[256,6,8,127]{3,2,1,0:T(8,128)}, f32[256,6,8,127]{3,2,1,0:T(8,128)}) fusion(bf16[256,6,8,128]{3,2,1,0:T(8,128)(2,1)S(1)} %fusion.31), kind=kLoop, calls=%fused_computation.178 | loop fusion | bytes 24969216 | tf_op jit(solution)/shard_map/jit(_roll_static)/slice | solution.py:65
  359.4 5.4 %fusion.100 = (f32[256,6,7,128]{3,2,1,0:T(8,128)}, f32[256,6,7,128]{3,2,1,0:T(8,128)}) fusion(bf16[256,6,8,128]{3,2,1,0:T(8,128)(2,1)S(1)} %fusion.31), kind=kLoop, calls=%fused_computation.176 | loop fusion | bytes 22020096 | tf_op jit(solution)/shard_map/jit(_roll_static)/slice | solution.py:60
  364.8 5.5 %fusion.101 = (f32[256,6,8,1]{3,2,1,0:T(8,128)}, f32[256,6,8,1]{3,2,1,0:T(8,128)}) fusion(bf16[256,6,8,128]{3,2,1,0:T(8,128)(2,1)S(1)} %fusion.31), kind=kLoop, calls=%fused_computation.177 | loop fusion | bytes 196608 | tf_op jit(solution)/shard_map/jit(_roll_static)/slice | solution.py:65
  370.3 4.7 %slice_convert_fusion.1 = (f32[256,5,8,128]{3,2,1,0:T(8,128)}, f32[256,5,8,128]{3,2,1,0:T(8,128)}) fusion(bf16[256,6,8,128]{3,2,1,0:T(8,128)(2,1)S(1)} %fusion.31), kind=kLoop, calls=%fused_computation.55 | loop fusion | flops 2621440 | bytes 15728640 | tf_op jit(solution)/shard_map/convert_element_type | solution.py:102
  374.9 0.0 collective-permute-done.2
  374.9 0.0 collective-permute-done.3
  374.9 3.6 fusion.45
  378.5 0.0 all-gather.5.cloned.1.call-done
  378.6 5.5 %fusion.108 = f32[6144,256]{1,0:T(8,128)} fusion(bf16[6144,256]{1,0:T(8,128)(2,1)} %all-gather.5.cloned.1.call-done, bf16[256,256]{1,0:T(8,128)(2,1)S(1)} %copy-done.3), kind=kOutput, calls=%fused_computation.184 | convolution fusion | flops 805306368 | bytes 9568256 | tf_op jit(solution)/shard_map/dot_general | solution.py:118
  384.0 6.7 %copy.15 = f32[256,6,8,128]{3,2,1,0:T(8,128)} copy(f32[256,6,8,128]{0,3,2,1:T(8,128)} %bitcast.78) | data formatting | bytes 12582912 | tf_op jit(solution)/shard_map/reshape | solution.py:123
  390.7 0.0 copy-start.1
  390.7 22.4 %fusion.30 = bf16[256,6,8,128]{3,2,1,0:T(8,128)(2,1)} fusion(f32[256,6,8,128]{3,2,1,0:T(8,128)} %copy.15, f32[256,6,8,1]{3,2,1,0:T(8,128)} %get-tuple-element.18, f32[256,6,8,127]{3,2,1,0:T(8,128)} %get-tuple-element.20, f32[256,6,8,127]{3,2,1,0:T(8,128)} %get-tuple-element.19, f32[256,6,8,1]{3,2,1,0:T(8,128)} %get-tuple-element.17, ...), kind=kLoop, calls=%fused_computation.46 | loop fusion | flops 48758784 | bytes 50338816 | tf_op jit(solution)/shard_map/convert_element_type | solution.py:129
  413.1 0.0 copy-done.1
  (8 shorter events, 0.1 us)
Async XLA Ops:
  6.5 0.9 copy-start
  6.5 98.0 %reduce-scatter.3.cloned.1.call-start = ((), (), s32[]{:S(2)}) async-start(), calls=%async_computation.2 | async-start | bytes 6684672 | tf_op jit(solution)/shard_map/reduce_scatter | solution.py:110
  13.3 93.0 %copy-start.2 = (bf16[256,6,8,128]{3,2,1,0:T(8,128)(2,1)S(1)}, bf16[256,6,8,128]{3,2,1,0:T(8,128)(2,1)}, u32[]{:S(2)}) copy-start(bf16[256,6,8,128]{3,2,1,0:T(8,128)(2,1)} %param.5) | copy-start | bytes 9437188
  13.3 166.5 %all-gather.3.cloned.1.call-start = ((), (), s32[]{:S(2)}) async-start(), calls=%async_computation.3 | async-start | bytes 3342336 | tf_op jit(solution)/shard_map/all_gather | solution.py:120
  106.2 199.3 %reduce-scatter.5.cloned.1.call-start = ((), (), s32[]{:S(2)}) async-start(), calls=%async_computation.4 | async-start | bytes 6684672 | tf_op jit(solution)/shard_map/reduce_scatter | solution.py:110
  107.4 67.2 %collective-permute-start = (bf16[256,1,8,128]{3,2,0,1:T(8,128)(2,1)}, bf16[256,1,8,128]{3,2,0,1:T(8,128)(2,1)}, u32[]{:S(2)}, u32[]{:S(2)}) collective-permute-start(bf16[256,1,8,128]{3,2,0,1:T(8,128)(2,1)} %get-tuple-element.21), channel_id=1, source_target_pairs={{0,16},{16,32},{32,48},{48,64},{64,80},{80,96},{96,112},{1,17},{17... | collective-permute-start | bytes 1572872 | tf_op jit(solution)/shard_map/ppermute | solution.py:18
  111.7 65.5 %collective-permute-start.1 = (bf16[256,1,8,128]{3,2,1,0:T(8,128)(2,1)}, bf16[256,1,8,128]{3,2,1,0:T(8,128)(2,1)}, u32[]{:S(2)}, u32[]{:S(2)}) collective-permute-start(bf16[256,1,8,128]{3,2,1,0:T(8,128)(2,1)} %get-tuple-element.22), channel_id=1, source_target_pairs={{16,0},{32,16},{48,32},{64,48},{80,64},{96,80},{112,96},{17,1},{33... | collective-permute-start | bytes 1572872 | tf_op jit(solution)/shard_map/ppermute | solution.py:21
  168.4 6.1 %copy-start.4 = (s32[2,8,128]{2,1,0:T(8,128)S(1)}, s32[2,8,128]{2,1,0:T(8,128)}, u32[]{:S(2)}) copy-start(s32[2,8,128]{2,1,0:T(8,128)} %param.9) | copy-start | bytes 24580
  168.4 11.4 %copy-start.3 = (bf16[256,256]{1,0:T(8,128)(2,1)S(1)}, bf16[256,256]{1,0:T(8,128)(2,1)}, u32[]{:S(2)}) copy-start(bf16[256,256]{1,0:T(8,128)(2,1)} %param.6) | copy-start | bytes 393220
  185.3 6.7 %copy-start.5 = (f32[256]{0:T(256)S(1)}, f32[256]{0:T(256)}, u32[]{:S(2)}) copy-start(f32[256]{0:T(256)} %param.8) | copy-start | bytes 3076
  217.8 160.8 %all-gather.5.cloned.1.call-start = ((), (), s32[]{:S(2)}) async-start(), calls=%async_computation.5 | async-start | bytes 3342336 | tf_op jit(solution)/shard_map/all_gather | solution.py:120
  308.3 66.6 %collective-permute-start.2 = (bf16[256,1,8,128]{3,2,0,1:T(8,128)(2,1)}, bf16[256,1,8,128]{3,2,0,1:T(8,128)(2,1)}, u32[]{:S(2)}, u32[]{:S(2)}) collective-permute-start(bf16[256,1,8,128]{3,2,0,1:T(8,128)(2,1)} %get-tuple-element.9), channel_id=1, source_target_pairs={{0,16},{16,32},{32,48},{48,64},{64,80},{80,96},{96,112},{1,17},{17... | collective-permute-start | bytes 1572872 | tf_op jit(solution)/shard_map/ppermute | solution.py:18
  312.7 62.3 %collective-permute-start.3 = (bf16[256,1,8,128]{3,2,0,1:T(8,128)(2,1)}, bf16[256,1,8,128]{3,2,0,1:T(8,128)(2,1)}, u32[]{:S(2)}, u32[]{:S(2)}) collective-permute-start(bf16[256,1,8,128]{3,2,0,1:T(8,128)(2,1)} %get-tuple-element.10), channel_id=1, source_target_pairs={{16,0},{32,16},{48,32},{64,48},{80,64},{96,80},{112,96},{17,1},{33... | collective-permute-start | bytes 1572872 | tf_op jit(solution)/shard_map/ppermute | solution.py:21
  390.7 22.4 %copy-start.1 = (bf16[256,256]{1,0:T(8,128)(2,1)S(1)}, bf16[256,256]{1,0:T(8,128)(2,1)}, u32[]{:S(2)}) copy-start(bf16[256,256]{1,0:T(8,128)(2,1)} %param.7) | copy-start | bytes 393220
Sparse Core Ops, SparseCore 0:
  13.5 91.0 reduce-scatter.2
  107.0 52.6 all-gather.2
  217.9 87.5 reduce-scatter.4
  307.9 52.6 all-gather.4
where the time goes:
time: 420 us
  waiting for transfers between devices  179 us (43%)
  blocking collectives  70 us (17%)
  other arithmetic  69.8 us (17%)
  local copies, waits for them, and re-layouts  53.4 us (13%)
  matrix products  20.8 us (5%)
  starting transfers between devices  13.4 us (3%)
  between operations  13.3 us (3%)
    reduce_scatter x2, waiting for transfers between devices, body(): lax.psum_scatter(lax.dot_general(flat_rows, down_factor, (((0,), (0,)), (...  179 us
    psum x2, blocking collectives, body(): outflux = lax.psum(jnp.stack([out_low, out_high]), 'vel')  70 us
    convert_element_type x2, other arithmetic, body(): current = updated.astype(jnp.bfloat16)  44.2 us
    slice x4, local copies, waits for them, and re-layouts, transport(): jnp.roll(centre, 1, axis_y)  22 us
    slice x4, local copies, waits for them, and re-layouts, transport(): jnp.roll(centre, 1, axis_x)  15 us
    reshape x2, local copies, waits for them, and re-layouts, body(): gained = lax.dot_general(up_factor, lax.all_gather(coeffs, 'vel', axis=0,...  13.4 us
    dot_general x2, matrix products, body(): lax.dot_general(up_factor, lax.all_gather(coeffs, 'vel', axis=0, tiled=Tr...  11 us
    dot_general x2, matrix products, body(): lax.dot_general(flat_rows, down_factor, (((0,), (0,)), ((), ())), preferr...  9.85 us
  transfers between devices with their start and end apart: 8, of which 2 were waited for; matrix products, arithmetic and copies ran while one was open for 15% of the time, Pallas kernels for 0%

commit v1 on v0

--- a/solution.py
+++ b/solution.py
@@ -90,7 +90,9 @@
         high_face = current[:, depth - 1].astype(jnp.float32)
         out_low = jnp.sum(jnp.maximum(-along_z, 0.0)[:, None, None] * low_face, axis=0)
         out_high = jnp.sum(jnp.maximum(along_z, 0.0)[:, None, None] * high_face, axis=0)
-        outflux = lax.psum(jnp.stack([out_low, out_high]), "vel")
+        x = jnp.stack([out_low, out_high])
+        parts = lax.all_gather(x, "vel", axis=0, tiled=False)
+        outflux = parts.sum(axis=0)
         ghost_low = wall_ghost(outflux[0], wall_kind[0], maxwell, energy, norm)
         ghost_high = wall_ghost(outflux[1], wall_kind[1], maxwell, energy, norm)
         padded = with_halo(current, (("space", 1),), 1)

time: 420 us -> 401 us (0.955)
  blocking collectives: 70 us -> 45.6 us
  waiting for transfers between devices: 179 us -> 186 us
    psum x2 -> x0, blocking collectives: 70 us -> none  [body(): outflux = lax.psum(jnp.stack([out_low, out_high]), 'vel')]
    all_gather x0 -> x2, blocking collectives: none -> 45.6 us  [body(): parts = lax.all_gather(x, 'vel', axis=0, tiled=False)]
    ppermute x2, waiting for transfers between devices: 0.01 us -> 7.03 us  [with_halo(): lax.ppermute(lax.slice_in_dim(block, 0, width, axis=dim), axis, backward)]
  transfers between devices with their start and end apart: 8 -> 8, of which waited for: 2 -> 3; matrix products, arithmetic and copies ran while one was open for 15% -> 15% of each run, Pallas kernels for 0% -> 0%
where the time goes in v1:
time: 401 us; the launch traced here: 400 us
  waiting for transfers between devices  186 us (46%)
  other arithmetic  68.8 us (17%)
  local copies, waits for them, and re-layouts  52.5 us (13%)
  blocking collectives  45.6 us (11%)
  matrix products  20.8 us (5%)
  between operations  13.3 us (3%)
  starting transfers between devices  12.6 us (3%)
    reduce_scatter x2, waiting for transfers between devices, body(): lax.psum_scatter(lax.dot_general(flat_rows, down_factor, (((0,), (0,)), (...  179 us
    all_gather x2, blocking collectives, body(): parts = lax.all_gather(x, 'vel', axis=0, tiled=False)  45.6 us
    convert_element_type x2, other arithmetic, body(): current = updated.astype(jnp.bfloat16)  44.4 us
    slice x4, local copies, waits for them, and re-layouts, transport(): jnp.roll(centre, 1, axis_y)  22 us
    slice x4, local copies, waits for them, and re-layouts, transport(): jnp.roll(centre, 1, axis_x)  15.1 us
    reshape x2, local copies, waits for them, and re-layouts, body(): gained = lax.dot_general(up_factor, lax.all_gather(coeffs, 'vel', axis=0,...  13.4 us
    dot_general x2, matrix products, body(): lax.dot_general(up_factor, lax.all_gather(coeffs, 'vel', axis=0, tiled=Tr...  11 us
    dot_general x2, matrix products, body(): lax.dot_general(flat_rows, down_factor, (((0,), (0,)), ((), ())), preferr...  9.85 us
  transfers between devices with their start and end apart: 8, of which 3 were waited for; matrix products, arithmetic and copies ran while one was open for 15% of the time, Pallas kernels for 0%

profile of v1, /device:TPU:8, one launch (start us, length us, event | category | flops | bytes accessed | tf_op | source)
XLA Modules:
  0.0 399.9 jit_solution(12482998584844061255)
XLA Ops:
  6.5 0.0 copy-start
  6.5 0.0 reduce-scatter.3.cloned.1.call-start
  6.5 0.9 copy-done
  7.4 5.9 %fusion.35 = f32[6144,256]{1,0:T(8,128)} fusion(bf16[256,256]{1,0:T(8,128)(2,1)S(1)} %copy-done, bf16[32,8,48,128]{3,2,1,0:T(8,128)(2,1)} %bitcast.78), kind=kOutput, calls=%fused_computation.51 | convolution fusion | flops 805306368 | bytes 9568256 | tf_op jit(solution)/shard_map/dot_general | solution.py:113
  13.3 0.0 copy-start.2
  13.3 0.0 reduce-scatter.3.cloned.1.call-update
  13.3 0.0 all-gather.5.cloned.1.call-start
  13.4 91.1 %reduce-scatter.3.cloned.1.call-done = f32[384,256]{1,0:T(8,128)} async-done(((f32[6144,256]{1,0:T(8,128)}), f32[384,256]{1,0:T(8,128)}) %reduce-scatter.3.cloned.1.call-update) | async-done | bytes 393232 | tf_op jit(solution)/shard_map/reduce_scatter | solution.py:112
  104.5 1.7 convert_element_type.151
  106.2 0.0 all-gather.5.cloned.1.call-update
  106.2 0.0 reduce-scatter.5.cloned.1.call-start
  106.3 0.0 copy-done.2
  106.3 1.1 slice_bitcast_fusion.2
  107.4 4.3 %collective-permute-start = (bf16[256,1,8,128]{3,2,0,1:T(8,128)(2,1)}, bf16[256,1,8,128]{3,2,0,1:T(8,128)(2,1)}, u32[]{:S(2)}, u32[]{:S(2)}) collective-permute-start(bf16[256,1,8,128]{3,2,0,1:T(8,128)(2,1)} %get-tuple-element.21), channel_id=1, source_target_pairs={{0,16},{16,32},{32,48},{48,64},{64,80},{80,96},{96,112},{1,17},{17... | collective-permute-start | bytes 1572872 | tf_op jit(solution)/shard_map/ppermute | solution.py:18
  111.7 2.3 collective-permute-start.1
  114.0 1.0 fusion.57
  115.0 23.0 %all-gather = f32[32,8,128]{2,1,0:T(8,128)S(1)} all-gather(f32[2,8,128]{2,1,0:T(8,128)S(1)} %pad_maximum_fusion), channel_id=2, replica_groups=mesh['space'=8,'vel'=16] {'vel'}, dimensions={0}, use_global_device_ids=true | all-gather | bytes 139264 | tf_op jit(solution)/shard_map/all_gather | solution.py:94
  138.1 0.7 fusion.86
  138.8 4.7 %slice_convert_fusion.3 = (f32[256,5,8,128]{3,2,1,0:T(8,128)}, f32[256,5,8,128]{3,2,1,0:T(8,128)}) fusion(bf16[256,6,8,128]{3,2,1,0:T(8,128)(2,1)S(1)} %copy-done.2), kind=kLoop, calls=%fused_computation.57 | loop fusion | flops 2621440 | bytes 15728640 | tf_op jit(solution)/shard_map/convert_element_type | solution.py:104
  143.5 2.1 fusion.103
  145.5 5.5 %fusion.106 = (f32[256,6,8,127]{3,2,1,0:T(8,128)}, f32[256,6,8,127]{3,2,1,0:T(8,128)}) fusion(bf16[256,6,8,128]{3,2,1,0:T(8,128)(2,1)S(1)} %copy-done.2), kind=kLoop, calls=%fused_computation.182 | loop fusion | bytes 24969216 | tf_op jit(solution)/shard_map/jit(_roll_static)/slice | solution.py:65
  151.0 5.6 %fusion.105 = (f32[256,6,8,1]{3,2,1,0:T(8,128)}, f32[256,6,8,1]{3,2,1,0:T(8,128)}) fusion(bf16[256,6,8,128]{3,2,1,0:T(8,128)(2,1)S(1)} %copy-done.2), kind=kLoop, calls=%fused_computation.181 | loop fusion | bytes 196608 | tf_op jit(solution)/shard_map/jit(_roll_static)/slice | solution.py:65
  156.6 0.0 copy-start.4
  156.6 0.0 copy-start.3
  156.6 5.4 %fusion.104 = (f32[256,6,7,128]{3,2,1,0:T(8,128)}, f32[256,6,7,128]{3,2,1,0:T(8,128)}) fusion(bf16[256,6,8,128]{3,2,1,0:T(8,128)(2,1)S(1)} %copy-done.2), kind=kLoop, calls=%fused_computation.180 | loop fusion | bytes 22020096 | tf_op jit(solution)/shard_map/jit(_roll_static)/slice | solution.py:60
  162.1 0.6 fusion.90
  162.7 0.0 copy-done.4
  162.7 0.0 collective-permute-done
  162.8 2.6 fusion.41
  165.4 0.0 collective-permute-done.1
  165.4 2.6 fusion.49
  168.0 0.0 all-gather.5.cloned.1.call-done
  168.0 0.0 copy-done.3
  168.0 5.5 %fusion.107 = f32[6144,256]{1,0:T(8,128)} fusion(bf16[6144,256]{1,0:T(8,128)(2,1)} %all-gather.5.cloned.1.call-done, bf16[256,256]{1,0:T(8,128)(2,1)S(1)} %copy-done.3), kind=kOutput, calls=%fused_computation.183 | convolution fusion | flops 805306368 | bytes 9568256 | tf_op jit(solution)/shard_map/dot_general | solution.py:120
  173.5 0.0 copy-start.5
  173.5 6.7 %copy.20 = f32[256,6,8,128]{3,2,1,0:T(8,128)} copy(f32[256,6,8,128]{0,3,2,1:T(8,128)} %bitcast.79) | data formatting | bytes 12582912 | tf_op jit(solution)/shard_map/reshape | solution.py:125
  180.2 0.0 copy-done.5
  180.2 22.0 %fusion.31 = bf16[256,6,8,128]{3,2,1,0:T(8,128)(2,1)S(1)} fusion(f32[256,6,8,128]{3,2,1,0:T(8,128)} %copy.20, f32[256,6,8,1]{3,2,1,0:T(8,128)} %get-tuple-element.30, f32[256,6,8,127]{3,2,1,0:T(8,128)} %get-tuple-element.32, f32[256,6,8,127]{3,2,1,0:T(8,128)} %get-tuple-element.31, f32[256,6,8,1]{3,2,1,0:T(8,128)} %get-tuple-element.29, ...), kind=kLoop, calls=%fused_computation.47 | loop fusion | flops 48758784 | bytes 50338816 | tf_op jit(solution)/shard_map/convert_element_type | solution.py:131
  202.2 4.0 fusion.32
  206.2 0.0 reduce-scatter.5.cloned.1.call-update
  206.2 0.0 all-gather.7.cloned.1.call-start
  206.2 88.0 %reduce-scatter.5.cloned.1.call-done = f32[384,256]{1,0:T(8,128)} async-done(((f32[6144,256]{1,0:T(8,128)}), f32[384,256]{1,0:T(8,128)}) %reduce-scatter.5.cloned.1.call-update) | async-done | bytes 393232 | tf_op jit(solution)/shard_map/reduce_scatter | solution.py:112
  294.2 1.7 convert_element_type.162
  295.9 0.0 all-gather.7.cloned.1.call-update
  296.0 1.0 fusion.55
  297.0 22.6 %all-gather.1 = f32[32,8,128]{2,1,0:T(8,128)S(1)} all-gather(f32[2,8,128]{2,1,0:T(8,128)S(1)} %pad_maximum_fusion.1), channel_id=3, replica_groups=mesh['space'=8,'vel'=16] {'vel'}, dimensions={0}, use_global_device_ids=true | all-gather | bytes 139264 | tf_op jit(solution)/shard_map/all_gather | solution.py:94
  319.6 0.1 slice_bitcast_fusion
  319.6 3.4 collective-permute-start.2
  323.0 2.5 collective-permute-start.3
  325.5 0.6 fusion.88
  326.2 2.1 fusion.99
  328.3 5.5 %fusion.102 = (f32[256,6,8,127]{3,2,1,0:T(8,128)}, f32[256,6,8,127]{3,2,1,0:T(8,128)}) fusion(bf16[256,6,8,128]{3,2,1,0:T(8,128)(2,1)S(1)} %fusion.31), kind=kLoop, calls=%fused_computation.178 | loop fusion | bytes 24969216 | tf_op jit(solution)/shard_map/jit(_roll_static)/slice | solution.py:65
  333.7 5.4 %fusion.100 = (f32[256,6,7,128]{3,2,1,0:T(8,128)}, f32[256,6,7,128]{3,2,1,0:T(8,128)}) fusion(bf16[256,6,8,128]{3,2,1,0:T(8,128)(2,1)S(1)} %fusion.31), kind=kLoop, calls=%fused_computation.176 | loop fusion | bytes 22020096 | tf_op jit(solution)/shard_map/jit(_roll_static)/slice | solution.py:60
  339.2 5.5 %fusion.101 = (f32[256,6,8,1]{3,2,1,0:T(8,128)}, f32[256,6,8,1]{3,2,1,0:T(8,128)}) fusion(bf16[256,6,8,128]{3,2,1,0:T(8,128)(2,1)S(1)} %fusion.31), kind=kLoop, calls=%fused_computation.177 | loop fusion | bytes 196608 | tf_op jit(solution)/shard_map/jit(_roll_static)/slice | solution.py:65
  344.7 4.7 %slice_convert_fusion.1 = (f32[256,5,8,128]{3,2,1,0:T(8,128)}, f32[256,5,8,128]{3,2,1,0:T(8,128)}) fusion(bf16[256,6,8,128]{3,2,1,0:T(8,128)(2,1)S(1)} %fusion.31), kind=kLoop, calls=%fused_computation.55 | loop fusion | flops 2621440 | bytes 15728640 | tf_op jit(solution)/shard_map/convert_element_type | solution.py:104
  349.4 0.0 collective-permute-done.2
  349.4 7.0 %collective-permute-done.3 = bf16[256,1,8,128]{3,2,0,1:T(8,128)(2,1)S(1)} collective-permute-done((bf16[256,1,8,128]{3,2,0,1:T(8,128)(2,1)S(1)}, bf16[256,1,8,128]{3,2,0,1:T(8,128)(2,1)S(1)}, u32[]{:S(2)}, u32[]{:S(2)}) %collective-permute-start.3) | collective-permute-done | bytes 524320 | tf_op jit(solution)/shard_map/ppermute | solution.py:21
  356.4 2.3 fusion.45
  358.8 0.0 all-gather.7.cloned.1.call-done
  358.8 5.5 %fusion.108 = f32[6144,256]{1,0:T(8,128)} fusion(bf16[6144,256]{1,0:T(8,128)(2,1)} %all-gather.7.cloned.1.call-done, bf16[256,256]{1,0:T(8,128)(2,1)S(1)} %copy-done.3), kind=kOutput, calls=%fused_computation.184 | convolution fusion | flops 805306368 | bytes 9568256 | tf_op jit(solution)/shard_map/dot_general | solution.py:120
  364.3 6.7 %copy.25 = f32[256,6,8,128]{3,2,1,0:T(8,128)} copy(f32[256,6,8,128]{0,3,2,1:T(8,128)} %bitcast.80) | data formatting | bytes 12582912 | tf_op jit(solution)/shard_map/reshape | solution.py:125
  370.9 0.0 copy-start.1
  370.9 22.4 %fusion.30 = bf16[256,6,8,128]{3,2,1,0:T(8,128)(2,1)} fusion(f32[256,6,8,128]{3,2,1,0:T(8,128)} %copy.25, f32[256,6,8,1]{3,2,1,0:T(8,128)} %get-tuple-element.18, f32[256,6,8,127]{3,2,1,0:T(8,128)} %get-tuple-element.20, f32[256,6,8,127]{3,2,1,0:T(8,128)} %get-tuple-element.19, f32[256,6,8,1]{3,2,1,0:T(8,128)} %get-tuple-element.17, ...), kind=kLoop, calls=%fused_computation.46 | loop fusion | flops 48758784 | bytes 50338816 | tf_op jit(solution)/shard_map/convert_element_type | solution.py:131
  393.4 0.0 copy-done.1
  (10 shorter events, 0.2 us)
Async XLA Ops:
  6.5 0.9 copy-start
  6.5 98.0 %reduce-scatter.3.cloned.1.call-start = ((), (), s32[]{:S(2)}) async-start(), calls=%async_computation.2 | async-start | bytes 6684672 | tf_op jit(solution)/shard_map/reduce_scatter | solution.py:112
  13.3 93.0 %copy-start.2 = (bf16[256,6,8,128]{3,2,1,0:T(8,128)(2,1)S(1)}, bf16[256,6,8,128]{3,2,1,0:T(8,128)(2,1)}, u32[]{:S(2)}) copy-start(bf16[256,6,8,128]{3,2,1,0:T(8,128)(2,1)} %param.5) | copy-start | bytes 9437188
  13.3 154.6 %all-gather.5.cloned.1.call-start = ((), (), s32[]{:S(2)}) async-start(), calls=%async_computation.3 | async-start | bytes 3342336 | tf_op jit(solution)/shard_map/all_gather | solution.py:122
  106.2 188.0 %reduce-scatter.5.cloned.1.call-start = ((), (), s32[]{:S(2)}) async-start(), calls=%async_computation.4 | async-start | bytes 6684672 | tf_op jit(solution)/shard_map/reduce_scatter | solution.py:112
  107.4 55.4 %collective-permute-start = (bf16[256,1,8,128]{3,2,0,1:T(8,128)(2,1)}, bf16[256,1,8,128]{3,2,0,1:T(8,128)(2,1)}, u32[]{:S(2)}, u32[]{:S(2)}) collective-permute-start(bf16[256,1,8,128]{3,2,0,1:T(8,128)(2,1)} %get-tuple-element.21), channel_id=1, source_target_pairs={{0,16},{16,32},{32,48},{48,64},{64,80},{80,96},{96,112},{1,17},{17... | collective-permute-start | bytes 1572872 | tf_op jit(solution)/shard_map/ppermute | solution.py:18
  111.7 53.7 %collective-permute-start.1 = (bf16[256,1,8,128]{3,2,1,0:T(8,128)(2,1)}, bf16[256,1,8,128]{3,2,1,0:T(8,128)(2,1)}, u32[]{:S(2)}, u32[]{:S(2)}) collective-permute-start(bf16[256,1,8,128]{3,2,1,0:T(8,128)(2,1)} %get-tuple-element.22), channel_id=1, source_target_pairs={{16,0},{32,16},{48,32},{64,48},{80,64},{96,80},{112,96},{17,1},{33... | collective-permute-start | bytes 1572872 | tf_op jit(solution)/shard_map/ppermute | solution.py:21
  156.6 6.1 %copy-start.4 = (s32[2,8,128]{2,1,0:T(8,128)S(1)}, s32[2,8,128]{2,1,0:T(8,128)}, u32[]{:S(2)}) copy-start(s32[2,8,128]{2,1,0:T(8,128)} %param.9) | copy-start | bytes 24580
  156.6 11.4 %copy-start.3 = (bf16[256,256]{1,0:T(8,128)(2,1)S(1)}, bf16[256,256]{1,0:T(8,128)(2,1)}, u32[]{:S(2)}) copy-start(bf16[256,256]{1,0:T(8,128)(2,1)} %param.6) | copy-start | bytes 393220
  173.5 6.7 %copy-start.5 = (f32[256]{0:T(256)S(1)}, f32[256]{0:T(256)}, u32[]{:S(2)}) copy-start(f32[256]{0:T(256)} %param.8) | copy-start | bytes 3076
  206.2 152.6 %all-gather.7.cloned.1.call-start = ((), (), s32[]{:S(2)}) async-start(), calls=%async_computation.5 | async-start | bytes 3342336 | tf_op jit(solution)/shard_map/all_gather | solution.py:122
  319.6 29.7 %collective-permute-start.2 = (bf16[256,1,8,128]{3,2,0,1:T(8,128)(2,1)S(1)}, bf16[256,1,8,128]{3,2,0,1:T(8,128)(2,1)S(1)}, u32[]{:S(2)}, u32[]{:S(2)}) collective-permute-start(bf16[256,1,8,128]{3,2,0,1:T(8,128)(2,1)S(1)} %get-tuple-element.9), channel_id=1, source_target_pairs={{0,16},{16,32},{32,48},{48,64},{64,80},{80,96},{96,112},{1,17},{17... | collective-permute-start | bytes 1572872 | tf_op jit(solution)/shard_map/ppermute | solution.py:18
  323.0 33.4 %collective-permute-start.3 = (bf16[256,1,8,128]{3,2,0,1:T(8,128)(2,1)S(1)}, bf16[256,1,8,128]{3,2,0,1:T(8,128)(2,1)S(1)}, u32[]{:S(2)}, u32[]{:S(2)}) collective-permute-start(bf16[256,1,8,128]{3,2,0,1:T(8,128)(2,1)S(1)} %get-tuple-element.10), channel_id=1, source_target_pairs={{16,0},{32,16},{48,32},{64,48},{80,64},{96,80},{112,96},{17,1},{33... | collective-permute-start | bytes 1572872 | tf_op jit(solution)/shard_map/ppermute | solution.py:21
  370.9 22.4 %copy-start.1 = (bf16[256,256]{1,0:T(8,128)(2,1)S(1)}, bf16[256,256]{1,0:T(8,128)(2,1)}, u32[]{:S(2)}) copy-start(bf16[256,256]{1,0:T(8,128)(2,1)} %param.7) | copy-start | bytes 393220
Sparse Core Ops, SparseCore 0:
  13.5 91.0 reduce-scatter.2
  107.0 52.7 all-gather.4
  206.3 87.8 reduce-scatter.4
  296.5 59.5 all-gather.6
